TPU v7x, 256 devices: a whole 4x4x8 slice. The times are simulated.
256 devices in a mesh: ha: 32 (over x_lo, z, core), wa: 8 (over x_hi, y).
Axes of the slice: x: 4 (x_hi: 2, x_lo: 2; x = x_hi * 2 + x_lo), y: 4, z: 8, core: 2. Of those that a mesh axis runs over, the one named last changes fastest.
Arguments:
- features: bfloat16 [256, 262144], P('ha', 'wa'), may hold values from -6 to 6
- grad_out: bfloat16 [256, 262144], P('ha', 'wa'), may hold values from -6 to 6
- dw_weight: float32 [49, 256], replicated, may hold values from -0.875 to 0.875
- dw_bias: float32 [256], replicated, may hold values from -3 to 3
- ln_gain: float32 [256], replicated, may hold values from 0.5 to 1.5
- ln_bias: float32 [256], replicated, may hold values from -3 to 3
- w_in: bfloat16 [256, 1024], replicated, may hold values from -0.375 to 0.375
- b_in: float32 [1024], replicated, may hold values from -3 to 3
- w_out: bfloat16 [1024, 256], replicated, may hold values from -0.1875 to 0.1875
- b_out: float32 [256], replicated, may hold values from -3 to 3
- scale: float32 [256], replicated, may hold values from 0.3 to 1.5
Outputs:
- grad_features: bfloat16 [256, 262144], P('ha', 'wa')
- clip_dw_weight: float32 [49, 256], replicated
- clip_dw_bias: float32 [256], replicated
- clip_ln_gain: float32 [256], replicated
- clip_ln_bias: float32 [256], replicated
- clip_w_in: float32 [256, 1024], replicated
- clip_b_in: float32 [1024], replicated
- clip_w_out: float32 [1024, 256], replicated
- clip_b_out: float32 [256], replicated
- clip_scale: float32 [256], replicated
All inputs are finite; a program needn't handle non-finite values.
Results may differ from a plain program's by a relative error of at most 0.0075.
Values may be sent and summed in bfloat16 or wider, within the bound.
No kernel may reach another device: no remote copies, remote signals or barrier semaphores. Data moves between devices by JAX's collectives and lax.ppermute only.
A program may use at most 64 MiB of HBM per device.

v0:
```python
import math
import jax
import jax.numpy as jnp
from jax import lax
from jax.sharding import PartitionSpec as P

eps_norm = 1e-06
clip_bound = 500.0


def with_halo(x, sides, width):
    for axis, dim in sides:
        devices, length = (lax.axis_size(axis), x.shape[dim])
        up = [(i, (i + 1) % devices) for i in range(devices - 1)]
        down = [(j, i) for i, j in up]
        last = lax.slice_in_dim(x, length - width, length, axis=dim)
        leading = lax.slice_in_dim(x, 0, width, axis=dim)
        before = lax.ppermute(last, axis, up)
        after = lax.ppermute(leading, axis, down)
        x = jnp.concatenate([before, x, after], axis=dim)
    return x


def gelu_parts(pre):
    cdf = 0.5 * (1.0 + jax.scipy.special.erf(pre / math.sqrt(2.0)))
    pdf = jnp.exp(-0.5 * pre * pre) / math.sqrt(2.0 * math.pi)
    return (pre * cdf, cdf + pre * pdf)


def conv_rows(padded, weight, rows, cols, flip):
    total = jnp.zeros((rows, cols, padded.shape[2]), jnp.float32)
    for first in range(7):
        for second in range(7):
            if flip:
                window = padded[6 - first : 6 - first + rows, 6 - second : 6 - second + cols]
            else:
                window = padded[first : first + rows, second : second + cols]
            total = total + window.astype(jnp.float32) * weight[first * 7 + second]
    return total


def contract_rows(left, right):
    return lax.dot_general(
        left, right, (((0,), (0,)), ((), ())), preferred_element_type=jnp.float32
    )


def block_backward(
    padded, grad, dw_weight, dw_bias, ln_gain, ln_bias, w_in, b_in, w_out, b_out, scale
):
    rows, cols, chans = grad.shape
    conv = conv_rows(padded, dw_weight, rows, cols, False) + dw_bias
    center = conv - jnp.mean(conv, axis=-1, keepdims=True)
    inverse = lax.rsqrt(jnp.mean(center * center, axis=-1, keepdims=True) + eps_norm)
    normed = (center * inverse).reshape(rows * cols, chans)
    inverse = inverse.reshape(rows * cols, 1)
    lnout = (normed * ln_gain + ln_bias).astype(jnp.bfloat16)
    pre = jnp.dot(lnout, w_in, preferred_element_type=jnp.float32) + b_in
    act_full, slope = gelu_parts(pre)
    act = act_full.astype(jnp.bfloat16)
    branch = jnp.dot(act, w_out, preferred_element_type=jnp.float32) + b_out
    gflat = grad.reshape(rows * cols, chans).astype(jnp.float32)
    g_scale = jnp.sum(gflat * branch, axis=0)
    dbranch = (gflat * scale).astype(jnp.bfloat16)
    g_wout = contract_rows(act, dbranch)
    g_bout = jnp.sum(dbranch.astype(jnp.float32), axis=0)
    dact = lax.dot_general(
        dbranch, w_out, (((1,), (1,)), ((), ())), preferred_element_type=jnp.float32
    )
    dpre = (dact * slope).astype(jnp.bfloat16)
    g_win_t = contract_rows(dpre, lnout)
    g_bin = jnp.sum(dpre.astype(jnp.float32), axis=0)
    dln = lax.dot_general(dpre, w_in, (((1,), (1,)), ((), ())), preferred_element_type=jnp.float32)
    g_gain = jnp.sum(dln * normed, axis=0)
    g_lnb = jnp.sum(dln, axis=0)
    dnorm = dln * ln_gain
    dconv_flat = (
        dnorm
        - jnp.mean(dnorm, axis=-1, keepdims=True)
        - normed * jnp.mean(dnorm * normed, axis=-1, keepdims=True)
    ) * inverse
    dconv = dconv_flat.astype(jnp.bfloat16).reshape(rows, cols, chans)
    dconv_wide = dconv.astype(jnp.float32)
    g_dwb = jnp.sum(dconv_wide, axis=(0, 1))
    kernel_terms = []
    for first in range(7):
        for second in range(7):
            window = padded[first : first + rows, second : second + cols].astype(jnp.float32)
            kernel_terms.append(jnp.sum(dconv_wide * window, axis=(0, 1)))
    g_dw = jnp.stack(kernel_terms)
    return (dconv, (g_dw, g_dwb, g_gain, g_lnb, g_win_t, g_bin, g_wout, g_bout, g_scale))


def on_device(
    features, grad_out, dw_weight, dw_bias, ln_gain, ln_bias, w_in, b_in, w_out, b_out, scale
):
    chans = dw_weight.shape[1]
    rows = features.shape[0]
    cols = features.shape[1] // chans
    image = features.reshape(rows, cols, chans)
    grads3 = grad_out.reshape(rows, cols, chans)
    padded = with_halo(image, (("ha", 0), ("wa", 1)), 3)
    dconv, terms = block_backward(
        padded, grads3, dw_weight, dw_bias, ln_gain, ln_bias, w_in, b_in, w_out, b_out, scale
    )
    dpad = with_halo(dconv, (("ha", 0), ("wa", 1)), 3)
    result = conv_rows(dpad, dw_weight, rows, cols, True) + grads3.astype(jnp.float32)
    grad_features = result.astype(jnp.bfloat16).reshape(rows, cols * chans)
    g_dw, g_dwb, g_gain, g_lnb, g_win_t, g_bin, g_wout, g_bout, g_scale = terms
    summed = lax.psum(
        (g_dw, g_dwb, g_gain, g_lnb, g_bin, g_bout, g_scale, g_win_t, g_wout), ("ha", "wa")
    )
    squares = sum((jnp.sum(t * t) for t in summed))
    factor = jnp.minimum(1.0, clip_bound / jnp.sqrt(squares))
    s_dw, s_dwb, s_gain, s_lnb, s_bin, s_bout, s_scale, s_win_t, s_wout = summed
    full_win_t = factor * s_win_t
    full_wout = factor * s_wout
    return (
        grad_features,
        factor * s_dw,
        factor * s_dwb,
        factor * s_gain,
        factor * s_lnb,
        full_win_t.T,
        factor * s_bin,
        full_wout,
        factor * s_bout,
        factor * s_scale,
    )


def solution(mesh):
    return jax.shard_map(
        on_device,
        mesh=mesh,
        in_specs=(P("ha", "wa"), P("ha", "wa"), P(), P(), P(), P(), P(), P(), P(), P(), P()),
        out_specs=(P("ha", "wa"), P(), P(), P(), P(), P(), P(), P(), P(), P()),
        check_vma=False,
    )
```

profile of v0, /device:TPU:2, one launch (start us, length us, event | category | flops | bytes accessed | tf_op | source)
XLA Modules:
  0.0 459.7 jit_solution(16799210369752203266)
XLA Ops:
  8.8 1.9 collective-permute-start
  11.4 7.2 %collective-permute-start.1 = (bf16[3,128,256]{2,1,0:T(8,128)(2,1)}, bf16[3,128,256]{2,1,0:T(8,128)(2,1)}, u32[]{:S(2)}, u32[]{:S(2)}) collective-permute-start(bf16[3,128,256]{2,1,0:T(8,128)(2,1)} %bitcast.196), channel_id=1, source_target_pairs={{8,0},{16,8},{24,16},{32,24},{40,32},{48,40},{56,48},{64,56},{72,6... | collective-permute-start | bytes 589832 | tf_op jit(solution)/shard_map/ppermute | solution.py:19
  18.6 1.7 fusion.191
  21.5 2.1 convert_reduce_fusion.2
  26.2 3.5 collective-permute-start.2
  32.8 2.1 convert_element_type.503
  35.5 13.0 %fusion.186 = (f32[8,128]{1,0:T(8,128)S(1)}, f32[8,128,256]{2,1,0:T(8,128)S(1)}) fusion(f32[256]{0:T(256)} %param.14, f32[256]{0:T(256)} %bitcast.304, bf16[14,3,256]{2,1,0:T(4,128)(2,1)S(1)} %collective-permute-done.3, bf16[14,128,256]{2,1,0:T(8,128)(2,1)S(1)} %get-tuple-element.110, f32[256]{0:T(256)} %bitcast.306, f32[256]{0:T(256)} %bitcast.212, ...), kind=kLoop, calls=%fused_computation.387 | loop fusion | flops 71826432 | bytes 5734400 | tf_op jit(solution)/shard_map/reduce_sum | solution.py:53
  49.4 1.7 multiply_convert_fusion
  51.1 3.1 convert_reduce_fusion
  54.2 1.7 fusion.194
  57.5 2.2 fusion.122
  61.5 1.7 fusion.195
  64.6 3.0 fusion.7
  74.1 1.8 fusion.125
  75.9 4.1 stack.199
  80.0 79.4 %all-reduce = (f32[49,256]{1,0:T(8,128)S(1)}, f32[256]{0:T(256)S(1)}, f32[256]{0:T(256)S(1)}, f32[256]{0:T(256)S(1)}, f32[1024]{0:T(1024)S(1)}, /*index=5*/f32[256]{0:T(256)S(1)}, f32[256]{0:T(256)S(1)}) all-reduce(f32[49,256]{1,0:T(8,128)S(1)} %stack.199, ...), channel_id=1, replica_groups=mesh['ha'=32,'wa'=8] {'ha','wa'}, use_global_device_ids=true, to_apply=%region_53.0 | all-reduce | flops 14848 | bytes 118784 | tf_op jit(solution)/shard_map/psum | solution.py:110
  161.8 1.9 collective-permute-start.4
  163.7 5.8 %collective-permute-start.5 = (bf16[3,128,256]{2,1,0:T(8,128)(2,1)S(1)}, bf16[3,128,256]{2,1,0:T(8,128)(2,1)S(1)}, u32[]{:S(2)}, u32[]{:S(2)}) collective-permute-start(bf16[3,128,256]{2,1,0:T(8,128)(2,1)S(1)} %bitcast.208), channel_id=1, source_target_pairs={{8,0},{16,8},{24,16},{32,24},{40,32},{48,40},{56,48},{64,56},{72,6... | collective-permute-start | bytes 589832 | tf_op jit(solution)/shard_map/ppermute | solution.py:19
  171.1 1.5 collective-permute-done.5
  174.0 4.5 collective-permute-start.7
  184.6 11.2 %fusion.183 = bf16[1,8,128,256]{3,2,1,0:T(8,128)(2,1)S(1)} fusion(f32[8,128,256]{2,0,1:T(8,128)S(1)} %bitcast.203, f32[256]{0:T(256)} %bitcast.305, bf16[14,131,256]{2,1,0:T(8,128)(2,1)S(1)} %get-tuple-element.95, f32[256]{0:T(256)} %bitcast.307, f32[256]{0:T(256)S(1)} %bitcast.213, f32[256]{0:T(256)S(1)} %bitcast.215, ...), kind=kLoop, calls=%fused_computation.355 | loop fusion | flops 40370176 | bytes 24560640
  196.9 244.4 %all-reduce.4.cloned.1.call-done = (f32[1024,256]{1,0:T(8,128)}, f32[1024,256]{1,0:T(8,128)}) async-done(((f32[1024,256]{1,0:T(8,128)}, f32[1024,256]{1,0:T(8,128)}), (f32[1024,256]{1,0:T(8,128)}, f32[1024,256]{1,0:T(8,128)})) %all-reduce.4.cloned.1.call-update) | async-done | bytes 2097168 | tf_op jit(solution)/shard_map/psum | solution.py:110
  441.4 2.5 multiply_reduce_fusion
  446.3 2.3 broadcast_multiply_fusion
  (162 shorter events, 34.6 us)
Async XLA Ops:
  7.2 434.1 %all-reduce.4.cloned.1.call-start = ((), (), s32[]{:S(2)}) async-start(), calls=%async_computation | async-start | bytes 4194304 | tf_op jit(solution)/shard_map/psum | solution.py:110
  8.8 15.6 %collective-permute-start = (bf16[3,128,256]{2,1,0:T(8,128)(2,1)S(1)}, bf16[3,128,256]{2,1,0:T(8,128)(2,1)S(1)}, u32[]{:S(2)}, u32[]{:S(2)}) collective-permute-start(bf16[3,128,256]{2,1,0:T(8,128)(2,1)S(1)} %bitcast.207), channel_id=1, source_target_pairs={{0,8},{8,16},{16,24},{24,32},{32,40},{40,48},{48,56},{56,64},{64,7... | collective-permute-start | bytes 589832 | tf_op jit(solution)/shard_map/ppermute | solution.py:18
  11.4 13.2 %collective-permute-start.1 = (bf16[3,128,256]{2,1,0:T(8,128)(2,1)}, bf16[3,128,256]{2,1,0:T(8,128)(2,1)}, u32[]{:S(2)}, u32[]{:S(2)}) collective-permute-start(bf16[3,128,256]{2,1,0:T(8,128)(2,1)} %bitcast.196), channel_id=1, source_target_pairs={{8,0},{16,8},{24,16},{32,24},{40,32},{48,40},{56,48},{64,56},{72,6... | collective-permute-start | bytes 589832 | tf_op jit(solution)/shard_map/ppermute | solution.py:19
  26.2 8.7 %collective-permute-start.2 = (bf16[14,3,256]{2,1,0:T(4,128)(2,1)}, bf16[14,3,256]{2,1,0:T(4,128)(2,1)S(1)}, u32[]{:S(2)}, u32[]{:S(2)}) collective-permute-start(bf16[14,3,256]{2,1,0:T(4,128)(2,1)} %get-tuple-element.98), channel_id=1, source_target_pairs={{0,1},{1,2},{2,3},{3,4},{4,5},{5,6},{6,7},{8,9},{9,10},{10,11},{11... | collective-permute-start | bytes 64520 | tf_op jit(solution)/shard_map/ppermute | solution.py:18
  29.7 5.8 %collective-permute-start.3 = (bf16[14,3,256]{2,1,0:T(4,128)(2,1)S(1)}, bf16[14,3,256]{2,1,0:T(4,128)(2,1)S(1)}, u32[]{:S(2)}, u32[]{:S(2)}) collective-permute-start(bf16[14,3,256]{2,1,0:T(4,128)(2,1)S(1)} %get-tuple-element.99), channel_id=1, source_target_pairs={{1,0},{2,1},{3,2},{4,3},{5,4},{6,5},{7,6},{9,8},{10,9},{11,10},{12... | collective-permute-start | bytes 64520 | tf_op jit(solution)/shard_map/ppermute | solution.py:19
  73.7 110.5 %copy-start.5 = (f32[8,32768]{1,0:T(8,128)S(1)}, f32[8,32768]{1,0:T(8,128)}, u32[]{:S(2)}) copy-start(f32[8,32768]{1,0:T(8,128)} %convert_element_type.503) | copy-start | bytes 3145732
  73.7 110.5 %copy-start.9 = (f32[1,256]{1,0:T(1,128)S(1)}, f32[1,256]{1,0:T(1,128)}, u32[]{:S(2)}) copy-start(f32[1,256]{1,0:T(1,128)} %get-tuple-element.112) | copy-start | bytes 3076
  73.7 110.5 %copy-start.10 = (f32[1,256]{1,0:T(1,128)S(1)}, f32[1,256]{1,0:T(1,128)}, u32[]{:S(2)}) copy-start(f32[1,256]{1,0:T(1,128)} %get-tuple-element.113) | copy-start | bytes 3076
  73.7 110.5 %copy-start.11 = (f32[1,256]{1,0:T(1,128)S(1)}, f32[1,256]{1,0:T(1,128)}, u32[]{:S(2)}) copy-start(f32[1,256]{1,0:T(1,128)} %get-tuple-element.114) | copy-start | bytes 3076
  73.8 110.5 %copy-start.12 = (f32[1,256]{1,0:T(1,128)S(1)}, f32[1,256]{1,0:T(1,128)}, u32[]{:S(2)}) copy-start(f32[1,256]{1,0:T(1,128)} %get-tuple-element.115) | copy-start | bytes 3076
  73.8 110.5 %copy-start.13 = (f32[1,256]{1,0:T(1,128)S(1)}, f32[1,256]{1,0:T(1,128)}, u32[]{:S(2)}) copy-start(f32[1,256]{1,0:T(1,128)} %get-tuple-element.116) | copy-start | bytes 3076
  73.8 110.5 %copy-start.14 = (f32[1,256]{1,0:T(1,128)S(1)}, f32[1,256]{1,0:T(1,128)}, u32[]{:S(2)}) copy-start(f32[1,256]{1,0:T(1,128)} %get-tuple-element.117) | copy-start | bytes 3076
  73.8 110.5 %copy-start.15 = (f32[1,256]{1,0:T(1,128)S(1)}, f32[1,256]{1,0:T(1,128)}, u32[]{:S(2)}) copy-start(f32[1,256]{1,0:T(1,128)} %get-tuple-element.118) | copy-start | bytes 3076
  73.8 110.5 %copy-start.16 = (f32[1,256]{1,0:T(1,128)S(1)}, f32[1,256]{1,0:T(1,128)}, u32[]{:S(2)}) copy-start(f32[1,256]{1,0:T(1,128)} %get-tuple-element.119) | copy-start | bytes 3076
  73.8 110.5 %copy-start.17 = (f32[1,256]{1,0:T(1,128)S(1)}, f32[1,256]{1,0:T(1,128)}, u32[]{:S(2)}) copy-start(f32[1,256]{1,0:T(1,128)} %get-tuple-element.120) | copy-start | bytes 3076
  73.8 110.5 %copy-start.18 = (f32[1,256]{1,0:T(1,128)S(1)}, f32[1,256]{1,0:T(1,128)}, u32[]{:S(2)}) copy-start(f32[1,256]{1,0:T(1,128)} %get-tuple-element.121) | copy-start | bytes 3076
  73.8 110.5 %copy-start.19 = (f32[1,256]{1,0:T(1,128)S(1)}, f32[1,256]{1,0:T(1,128)}, u32[]{:S(2)}) copy-start(f32[1,256]{1,0:T(1,128)} %get-tuple-element.122) | copy-start | bytes 3076
  73.8 110.5 %copy-start.20 = (f32[1,256]{1,0:T(1,128)S(1)}, f32[1,256]{1,0:T(1,128)}, u32[]{:S(2)}) copy-start(f32[1,256]{1,0:T(1,128)} %get-tuple-element.123) | copy-start | bytes 3076
  73.8 110.5 %copy-start.21 = (f32[1,256]{1,0:T(1,128)S(1)}, f32[1,256]{1,0:T(1,128)}, u32[]{:S(2)}) copy-start(f32[1,256]{1,0:T(1,128)} %get-tuple-element.124) | copy-start | bytes 3076
  73.9 110.5 %copy-start.22 = (f32[1,256]{1,0:T(1,128)S(1)}, f32[1,256]{1,0:T(1,128)}, u32[]{:S(2)}) copy-start(f32[1,256]{1,0:T(1,128)} %get-tuple-element.125) | copy-start | bytes 3076
  161.8 9.3 %collective-permute-start.4 = (bf16[3,128,256]{2,1,0:T(8,128)(2,1)}, bf16[3,128,256]{2,1,0:T(8,128)(2,1)S(1)}, u32[]{:S(2)}, u32[]{:S(2)}) collective-permute-start(bf16[3,128,256]{2,1,0:T(8,128)(2,1)} %bitcast.209), channel_id=1, source_target_pairs={{0,8},{8,16},{16,24},{24,32},{32,40},{40,48},{48,56},{56,64},{64,7... | collective-permute-start | bytes 589832 | tf_op jit(solution)/shard_map/ppermute | solution.py:18
  163.7 8.9 %collective-permute-start.5 = (bf16[3,128,256]{2,1,0:T(8,128)(2,1)S(1)}, bf16[3,128,256]{2,1,0:T(8,128)(2,1)S(1)}, u32[]{:S(2)}, u32[]{:S(2)}) collective-permute-start(bf16[3,128,256]{2,1,0:T(8,128)(2,1)S(1)} %bitcast.208), channel_id=1, source_target_pairs={{8,0},{16,8},{24,16},{32,24},{40,32},{48,40},{56,48},{64,56},{72,6... | collective-permute-start | bytes 589832 | tf_op jit(solution)/shard_map/ppermute | solution.py:19
  172.7 11.0 %collective-permute-start.6 = (bf16[14,3,256]{2,1,0:T(4,128)(2,1)S(1)}, bf16[14,3,256]{2,1,0:T(4,128)(2,1)S(1)}, u32[]{:S(2)}, u32[]{:S(2)}) collective-permute-start(bf16[14,3,256]{2,1,0:T(4,128)(2,1)S(1)} %get-tuple-element.96), channel_id=1, source_target_pairs={{1,0},{2,1},{3,2},{4,3},{5,4},{6,5},{7,6},{9,8},{10,9},{11,10},{12... | collective-permute-start | bytes 64520 | tf_op jit(solution)/shard_map/ppermute | solution.py:19
  174.0 9.7 %collective-permute-start.7 = (bf16[14,3,256]{2,1,0:T(4,128)(2,1)S(1)}, bf16[14,3,256]{2,1,0:T(4,128)(2,1)S(1)}, u32[]{:S(2)}, u32[]{:S(2)}) collective-permute-start(bf16[14,3,256]{2,1,0:T(4,128)(2,1)S(1)} %get-tuple-element.97), channel_id=1, source_target_pairs={{0,1},{1,2},{2,3},{3,4},{4,5},{5,6},{6,7},{8,9},{9,10},{10,11},{11... | collective-permute-start | bytes 64520 | tf_op jit(solution)/shard_map/ppermute | solution.py:18
  (38 other events, 2911.9 us)
Sparse Core Ops, SparseCore 0:
  179.3 262.0 all-reduce.3
where the time goes:
time: 461 us; the launch traced here: 460 us
  waiting for transfers between devices  247 us (54%)
  blocking collectives  79.4 us (17%)
  other arithmetic  55.6 us (12%)
  starting transfers between devices  27.4 us (6%)
  between operations  20.9 us (5%)
  local copies, waits for them, and re-layouts  16.9 us (4%)
  matrix products  12.7 us (3%)
    psum x1, waiting for transfers between devices, on_device(): lax.psum((g_dw, g_dwb, g_gain, g_lnb, g_bin, g_bout, g_scale, g_win_t, g_...  244 us
    psum x1, blocking collectives, on_device(): lax.psum((g_dw, g_dwb, g_gain, g_lnb, g_bin, g_bout, g_scale, g_win_t, g_...  79.4 us
    ppermute x4, starting transfers between devices, with_halo(): after = lax.ppermute(leading, axis, down)  15.5 us
    reduce_sum x1, other arithmetic, block_backward(): center = conv - jnp.mean(conv, axis=-1, keepdims=True)  13 us
    ppermute x4, starting transfers between devices, with_halo(): before = lax.ppermute(last, axis, up)  11.8 us
    unnamed x1, other arithmetic  11.2 us
    reduce_sum x8, other arithmetic, block_backward(): kernel_terms.append(jnp.sum(dconv_wide * window, axis=(0, 1)))  11.2 us
  transfers between devices with their start and end apart: 9, of which 4 were waited for; matrix products, arithmetic and copies ran while one was open for 5% of the time, Pallas kernels for 0%

commit v1 on v0

--- a/solution.py
+++ b/solution.py
@@ -108,7 +108,7 @@
     grad_features = result.astype(jnp.bfloat16).reshape(rows, cols * chans)
     g_dw, g_dwb, g_gain, g_lnb, g_win_t, g_bin, g_wout, g_bout, g_scale = terms
     summed = lax.psum(
-        (g_dw, g_dwb, g_gain, g_lnb, g_bin, g_bout, g_scale, g_win_t, g_wout), ("ha", "wa")
+        lax.psum((g_dw, g_dwb, g_gain, g_lnb, g_bin, g_bout, g_scale, g_win_t, g_wout), "ha"), "wa"
     )
     squares = sum((jnp.sum(t * t) for t in summed))
     factor = jnp.minimum(1.0, clip_bound / jnp.sqrt(squares))

time: 461 us -> 420 us (0.911)
  waiting for transfers between devices: 247 us -> 135 us
  blocking collectives: 79.4 us -> 148 us
    psum x1, waiting for transfers between devices: 244 us -> 62.1 us  [on_device(): lax.psum((g_dw, g_dwb, g_gain, g_lnb, g_bin, g_bout, g_scale, g_win_t, g_...]
    psum x0 -> x1, waiting for transfers between devices: none -> 72.5 us  [on_device(): lax.psum(lax.psum((g_dw, g_dwb, g_gain, g_lnb, g_bin, g_bout, g_scale, g_...]
    psum x0 -> x1, blocking collectives: none -> 43 us  [on_device(): lax.psum(lax.psum((g_dw, g_dwb, g_gain, g_lnb, g_bin, g_bout, g_scale, g_...]
    psum x1, blocking collectives: 79.4 us -> 105 us  [on_device(): lax.psum((g_dw, g_dwb, g_gain, g_lnb, g_bin, g_bout, g_scale, g_win_t, g_...]
  transfers between devices with their start and end apart: 9 -> 10, of which waited for: 4 -> 3; matrix products, arithmetic and copies ran while one was open for 5% -> 11% of each run, Pallas kernels for 0% -> 0%
where the time goes in v1:
time: 420 us; the launch traced here: 419 us
  blocking collectives  148 us (35%)
  waiting for transfers between devices  135 us (32%)
  other arithmetic  57.7 us (14%)
  starting transfers between devices  27.6 us (7%)
  between operations  20.7 us (5%)
  local copies, waits for them, and re-layouts  17 us (4%)
  matrix products  12.8 us (3%)
    psum x1, blocking collectives, on_device(): lax.psum((g_dw, g_dwb, g_gain, g_lnb, g_bin, g_bout, g_scale, g_win_t, g_...  105 us
    psum x1, waiting for transfers between devices, on_device(): lax.psum(lax.psum((g_dw, g_dwb, g_gain, g_lnb, g_bin, g_bout, g_scale, g_...  72.5 us
    psum x1, waiting for transfers between devices, on_device(): lax.psum((g_dw, g_dwb, g_gain, g_lnb, g_bin, g_bout, g_scale, g_win_t, g_...  62.1 us
    psum x1, blocking collectives, on_device(): lax.psum(lax.psum((g_dw, g_dwb, g_gain, g_lnb, g_bin, g_bout, g_scale, g_...  43 us
    ppermute x4, starting transfers between devices, with_halo(): after = lax.ppermute(leading, axis, down)  15.5 us
    reduce_sum x1, other arithmetic, block_backward(): center = conv - jnp.mean(conv, axis=-1, keepdims=True)  13 us
    reduce_sum x8, other arithmetic, block_backward(): kernel_terms.append(jnp.sum(dconv_wide * window, axis=(0, 1)))  12.2 us
    ppermute x4, starting transfers between devices, with_halo(): before = lax.ppermute(last, axis, up)  11.9 us
  transfers between devices with their start and end apart: 10, of which 3 were waited for; matrix products, arithmetic and copies ran while one was open for 11% of the time, Pallas kernels for 0%

profile of v1, /device:TPU:2, one launch (start us, length us, event | category | flops | bytes accessed | tf_op | source)
XLA Modules:
  0.0 418.7 jit_solution(5786791283437492470)
XLA Ops:
  8.8 1.9 collective-permute-start
  11.4 7.2 %collective-permute-start.1 = (bf16[3,128,256]{2,1,0:T(8,128)(2,1)}, bf16[3,128,256]{2,1,0:T(8,128)(2,1)}, u32[]{:S(2)}, u32[]{:S(2)}) collective-permute-start(bf16[3,128,256]{2,1,0:T(8,128)(2,1)} %bitcast.196), channel_id=1, source_target_pairs={{8,0},{16,8},{24,16},{32,24},{40,32},{48,40},{56,48},{64,56},{72,6... | collective-permute-start | bytes 589832 | tf_op jit(solution)/shard_map/ppermute | solution.py:19
  21.5 2.1 convert_reduce_fusion.2
  26.2 3.5 collective-permute-start.2
  32.8 2.1 convert_element_type.503
  35.5 13.0 %fusion.186 = (f32[8,128]{1,0:T(8,128)S(1)}, f32[8,128,256]{2,1,0:T(8,128)S(1)}) fusion(f32[256]{0:T(256)} %param.14, f32[256]{0:T(256)} %bitcast.302, bf16[14,3,256]{2,1,0:T(4,128)(2,1)S(1)} %collective-permute-done.3, bf16[14,128,256]{2,1,0:T(8,128)(2,1)S(1)} %get-tuple-element.119, f32[256]{0:T(256)} %bitcast.304, f32[256]{0:T(256)} %bitcast.210, ...), kind=kLoop, calls=%fused_computation.387 | loop fusion | flops 71826432 | bytes 5734400 | tf_op jit(solution)/shard_map/reduce_sum | solution.py:53
  51.2 2.5 convert_reduce_fusion
  53.7 1.8 fusion.194
  55.4 2.4 fusion.136
  57.8 1.7 fusion.195
  59.5 3.4 fusion.122
  63.9 1.9 collective-permute-start.4
  65.9 5.8 %collective-permute-start.5 = (bf16[3,128,256]{2,1,0:T(8,128)(2,1)}, bf16[3,128,256]{2,1,0:T(8,128)(2,1)}, u32[]{:S(2)}, u32[]{:S(2)}) collective-permute-start(bf16[3,128,256]{2,1,0:T(8,128)(2,1)} %bitcast.54), channel_id=1, source_target_pairs={{8,0},{16,8},{24,16},{32,24},{40,32},{48,40},{56,48},{64,56},{72,6... | collective-permute-start | bytes 589832 | tf_op jit(solution)/shard_map/ppermute | solution.py:19
  80.7 4.1 stack.199
  84.9 2.8 fusion.7
  88.1 104.7 %all-reduce = (f32[49,256]{1,0:T(8,128)S(1)}, f32[256]{0:T(256)S(1)}, f32[256]{0:T(256)S(1)}, f32[256]{0:T(256)S(1)}, f32[1024]{0:T(1024)S(1)}, /*index=5*/f32[256]{0:T(256)S(1)}, f32[256]{0:T(256)S(1)}) all-reduce(f32[49,256]{1,0:T(8,128)S(1)} %stack.199, f32[256]{0:T(256)S(1)} %get-tuple-element.75, ...), channel_id=1, replica_groups=mesh['ha'=32,'wa'=8] {'ha'}, use_global_device_ids=true, to_apply=%region_53.0 | all-reduce | flops 14848 | bytes 118784 | tf_op jit(solution)/shard_map/psum | solution.py:111
  192.8 43.0 %all-reduce.2 = (f32[49,256]{1,0:T(8,128)S(1)}, f32[256]{0:T(256)S(1)}, f32[256]{0:T(256)S(1)}, f32[256]{0:T(256)S(1)}, f32[1024]{0:T(1024)S(1)}, /*index=5*/f32[256]{0:T(256)S(1)}, f32[256]{0:T(256)S(1)}) all-reduce(f32[49,256]{1,0:T(8,128)S(1)} %get-tuple-element.80, ...), channel_id=1, replica_groups=mesh['ha'=32,'wa'=8] {'wa'}, use_global_device_ids=true, to_apply=%region_54.0 | all-reduce | flops 14848 | bytes 118784 | tf_op jit(solution)/shard_map/psum | solution.py:110
  238.9 62.1 %all-reduce.7.cloned.1.call-done = (f32[1024,256]{1,0:T(8,128)}, f32[1024,256]{1,0:T(8,128)}) async-done(((f32[1024,256]{1,0:T(8,128)}, f32[1024,256]{1,0:T(8,128)}), (f32[1024,256]{1,0:T(8,128)}, f32[1024,256]{1,0:T(8,128)})) %all-reduce.7.cloned.1.call-update) | async-done | bytes 2097168 | tf_op jit(solution)/shard_map/psum | solution.py:111
  303.7 4.5 %collective-permute-start.7 = (bf16[14,3,256]{2,1,0:T(4,128)(2,1)S(1)}, bf16[14,3,256]{2,1,0:T(4,128)(2,1)S(1)}, u32[]{:S(2)}, u32[]{:S(2)}) collective-permute-start(bf16[14,3,256]{2,1,0:T(4,128)(2,1)S(1)} %get-tuple-element.106), channel_id=1, source_target_pairs={{0,1},{1,2},{2,3},{3,4},{4,5},{5,6},{6,7},{8,9},{9,10},{10,11},{11... | collective-permute-start | bytes 64520 | tf_op jit(solution)/shard_map/ppermute | solution.py:18
  313.2 1.7 pad_maximum_fusion
  315.3 11.5 %fusion.183 = bf16[1,8,128,256]{3,2,1,0:T(8,128)(2,1)S(1)} fusion(f32[8,128,256]{2,0,1:T(8,128)S(1)} %bitcast.203, f32[256]{0:T(256)} %bitcast.303, bf16[14,131,256]{2,1,0:T(8,128)(2,1)S(1)} %get-tuple-element.104, f32[256]{0:T(256)} %bitcast.305, f32[256]{0:T(256)S(1)} %bitcast.211, f32[256]{0:T(256)S(1)} %bitcast.213, ...), kind=kLoop, calls=%fused_computation.355 | loop fusion | flops 40370176 | bytes 24560640
  327.9 72.5 %all-reduce.9.cloned.1.call-done = (f32[1024,256]{1,0:T(8,128)}, f32[1024,256]{1,0:T(8,128)}) async-done(((f32[1024,256]{1,0:T(8,128)}, f32[1024,256]{1,0:T(8,128)}), (f32[1024,256]{1,0:T(8,128)}, f32[1024,256]{1,0:T(8,128)})) %all-reduce.9.cloned.1.call-update) | async-done | bytes 2097168 | tf_op jit(solution)/shard_map/psum | solution.py:110
  400.3 2.5 multiply_reduce_fusion
  405.3 2.3 broadcast_multiply_fusion
  (166 shorter events, 37.1 us)
Async XLA Ops:
  7.2 293.8 %all-reduce.7.cloned.1.call-start = ((), (), s32[]{:S(2)}) async-start(), calls=%async_computation | async-start | bytes 4194304 | tf_op jit(solution)/shard_map/psum | solution.py:111
  8.8 15.6 %collective-permute-start = (bf16[3,128,256]{2,1,0:T(8,128)(2,1)S(1)}, bf16[3,128,256]{2,1,0:T(8,128)(2,1)S(1)}, u32[]{:S(2)}, u32[]{:S(2)}) collective-permute-start(bf16[3,128,256]{2,1,0:T(8,128)(2,1)S(1)} %bitcast.207), channel_id=1, source_target_pairs={{0,8},{8,16},{16,24},{24,32},{32,40},{40,48},{48,56},{56,64},{64,7... | collective-permute-start | bytes 589832 | tf_op jit(solution)/shard_map/ppermute | solution.py:18
  11.4 13.2 %collective-permute-start.1 = (bf16[3,128,256]{2,1,0:T(8,128)(2,1)}, bf16[3,128,256]{2,1,0:T(8,128)(2,1)}, u32[]{:S(2)}, u32[]{:S(2)}) collective-permute-start(bf16[3,128,256]{2,1,0:T(8,128)(2,1)} %bitcast.196), channel_id=1, source_target_pairs={{8,0},{16,8},{24,16},{32,24},{40,32},{48,40},{56,48},{64,56},{72,6... | collective-permute-start | bytes 589832 | tf_op jit(solution)/shard_map/ppermute | solution.py:19
  26.2 8.7 %collective-permute-start.2 = (bf16[14,3,256]{2,1,0:T(4,128)(2,1)}, bf16[14,3,256]{2,1,0:T(4,128)(2,1)S(1)}, u32[]{:S(2)}, u32[]{:S(2)}) collective-permute-start(bf16[14,3,256]{2,1,0:T(4,128)(2,1)} %get-tuple-element.107), channel_id=1, source_target_pairs={{0,1},{1,2},{2,3},{3,4},{4,5},{5,6},{6,7},{8,9},{9,10},{10,11},{11... | collective-permute-start | bytes 64520 | tf_op jit(solution)/shard_map/ppermute | solution.py:18
  29.7 5.8 %collective-permute-start.3 = (bf16[14,3,256]{2,1,0:T(4,128)(2,1)S(1)}, bf16[14,3,256]{2,1,0:T(4,128)(2,1)S(1)}, u32[]{:S(2)}, u32[]{:S(2)}) collective-permute-start(bf16[14,3,256]{2,1,0:T(4,128)(2,1)S(1)} %get-tuple-element.108), channel_id=1, source_target_pairs={{1,0},{2,1},{3,2},{4,3},{5,4},{6,5},{7,6},{9,8},{10,9},{11,10},{12... | collective-permute-start | bytes 64520 | tf_op jit(solution)/shard_map/ppermute | solution.py:19
  63.9 237.7 %collective-permute-start.4 = (bf16[3,128,256]{2,1,0:T(8,128)(2,1)}, bf16[3,128,256]{2,1,0:T(8,128)(2,1)}, u32[]{:S(2)}, u32[]{:S(2)}) collective-permute-start(bf16[3,128,256]{2,1,0:T(8,128)(2,1)} %bitcast.52), channel_id=1, source_target_pairs={{0,8},{8,16},{16,24},{24,32},{32,40},{40,48},{48,56},{56,64},{64,7... | collective-permute-start | bytes 589832 | tf_op jit(solution)/shard_map/ppermute | solution.py:18
  65.9 235.8 %collective-permute-start.5 = (bf16[3,128,256]{2,1,0:T(8,128)(2,1)}, bf16[3,128,256]{2,1,0:T(8,128)(2,1)}, u32[]{:S(2)}, u32[]{:S(2)}) collective-permute-start(bf16[3,128,256]{2,1,0:T(8,128)(2,1)} %bitcast.54), channel_id=1, source_target_pairs={{8,0},{16,8},{24,16},{32,24},{40,32},{48,40},{56,48},{64,56},{72,6... | collective-permute-start | bytes 589832 | tf_op jit(solution)/shard_map/ppermute | solution.py:19
  71.6 328.7 %all-reduce.9.cloned.1.call-start = ((), (), s32[]{:S(2)}) async-start(), calls=%async_computation.1 | async-start | bytes 4194304 | tf_op jit(solution)/shard_map/psum | solution.py:110
  87.7 227.3 %copy-start.6 = (f32[8,32768]{1,0:T(8,128)S(1)}, f32[8,32768]{1,0:T(8,128)}, u32[]{:S(2)}) copy-start(f32[8,32768]{1,0:T(8,128)} %convert_element_type.503) | copy-start | bytes 3145732
  87.7 227.3 %copy-start.10 = (f32[1,256]{1,0:T(1,128)S(1)}, f32[1,256]{1,0:T(1,128)}, u32[]{:S(2)}) copy-start(f32[1,256]{1,0:T(1,128)} %get-tuple-element.121) | copy-start | bytes 3076
  87.7 227.3 %copy-start.11 = (f32[1,256]{1,0:T(1,128)S(1)}, f32[1,256]{1,0:T(1,128)}, u32[]{:S(2)}) copy-start(f32[1,256]{1,0:T(1,128)} %get-tuple-element.122) | copy-start | bytes 3076
  87.7 227.3 %copy-start.12 = (f32[1,256]{1,0:T(1,128)S(1)}, f32[1,256]{1,0:T(1,128)}, u32[]{:S(2)}) copy-start(f32[1,256]{1,0:T(1,128)} %get-tuple-element.123) | copy-start | bytes 3076
  87.7 227.3 %copy-start.13 = (f32[1,256]{1,0:T(1,128)S(1)}, f32[1,256]{1,0:T(1,128)}, u32[]{:S(2)}) copy-start(f32[1,256]{1,0:T(1,128)} %get-tuple-element.124) | copy-start | bytes 3076
  87.7 227.3 %copy-start.14 = (f32[1,256]{1,0:T(1,128)S(1)}, f32[1,256]{1,0:T(1,128)}, u32[]{:S(2)}) copy-start(f32[1,256]{1,0:T(1,128)} %get-tuple-element.125) | copy-start | bytes 3076
  87.7 227.3 %copy-start.15 = (f32[1,256]{1,0:T(1,128)S(1)}, f32[1,256]{1,0:T(1,128)}, u32[]{:S(2)}) copy-start(f32[1,256]{1,0:T(1,128)} %get-tuple-element.126) | copy-start | bytes 3076
  87.7 227.3 %copy-start.16 = (f32[1,256]{1,0:T(1,128)S(1)}, f32[1,256]{1,0:T(1,128)}, u32[]{:S(2)}) copy-start(f32[1,256]{1,0:T(1,128)} %get-tuple-element.127) | copy-start | bytes 3076
  87.7 227.3 %copy-start.17 = (f32[1,256]{1,0:T(1,128)S(1)}, f32[1,256]{1,0:T(1,128)}, u32[]{:S(2)}) copy-start(f32[1,256]{1,0:T(1,128)} %get-tuple-element.128) | copy-start | bytes 3076
  87.7 227.3 %copy-start.18 = (f32[1,256]{1,0:T(1,128)S(1)}, f32[1,256]{1,0:T(1,128)}, u32[]{:S(2)}) copy-start(f32[1,256]{1,0:T(1,128)} %get-tuple-element.129) | copy-start | bytes 3076
  87.8 227.3 %copy-start.19 = (f32[1,256]{1,0:T(1,128)S(1)}, f32[1,256]{1,0:T(1,128)}, u32[]{:S(2)}) copy-start(f32[1,256]{1,0:T(1,128)} %get-tuple-element.130) | copy-start | bytes 3076
  87.8 227.3 %copy-start.20 = (f32[1,256]{1,0:T(1,128)S(1)}, f32[1,256]{1,0:T(1,128)}, u32[]{:S(2)}) copy-start(f32[1,256]{1,0:T(1,128)} %get-tuple-element.131) | copy-start | bytes 3076
  87.8 227.3 %copy-start.21 = (f32[1,256]{1,0:T(1,128)S(1)}, f32[1,256]{1,0:T(1,128)}, u32[]{:S(2)}) copy-start(f32[1,256]{1,0:T(1,128)} %get-tuple-element.132) | copy-start | bytes 3076
  87.8 227.3 %copy-start.22 = (f32[1,256]{1,0:T(1,128)S(1)}, f32[1,256]{1,0:T(1,128)}, u32[]{:S(2)}) copy-start(f32[1,256]{1,0:T(1,128)} %get-tuple-element.133) | copy-start | bytes 3076
  302.4 10.8 %collective-permute-start.6 = (bf16[14,3,256]{2,1,0:T(4,128)(2,1)S(1)}, bf16[14,3,256]{2,1,0:T(4,128)(2,1)S(1)}, u32[]{:S(2)}, u32[]{:S(2)}) collective-permute-start(bf16[14,3,256]{2,1,0:T(4,128)(2,1)S(1)} %get-tuple-element.105), channel_id=1, source_target_pairs={{1,0},{2,1},{3,2},{4,3},{5,4},{6,5},{7,6},{9,8},{10,9},{11,10},{12... | collective-permute-start | bytes 64520 | tf_op jit(solution)/shard_map/ppermute | solution.py:19
  303.7 9.5 %collective-permute-start.7 = (bf16[14,3,256]{2,1,0:T(4,128)(2,1)S(1)}, bf16[14,3,256]{2,1,0:T(4,128)(2,1)S(1)}, u32[]{:S(2)}, u32[]{:S(2)}) collective-permute-start(bf16[14,3,256]{2,1,0:T(4,128)(2,1)S(1)} %get-tuple-element.106), channel_id=1, source_target_pairs={{0,1},{1,2},{2,3},{3,4},{4,5},{5,6},{6,7},{8,9},{9,10},{10,11},{11... | collective-permute-start | bytes 64520 | tf_op jit(solution)/shard_map/ppermute | solution.py:18
  (39 other events, 6057.8 us)
Sparse Core Ops, SparseCore 0:
  71.8 229.1 all-reduce.6
  303.9 96.3 all-reduce.8
